TPU v7x, 256 devices: a whole 4x4x8 slice. The times are simulated.
256 devices in a mesh: rep: 32 (over y, x, core), fsdp: 8 (over z).
Axes of the slice: x: 4, y: 4, z: 8, core: 2. Of those that a mesh axis runs over, the one named last changes fastest.
Arguments:
- codes: bfloat16 [32, 4096, 1024], P('rep', 'fsdp'), may hold values from -127 to 127
- block_scales: float32 [32, 4096, 8], P('rep', 'fsdp'), may hold values from 0.002 to 0.02
- params: bfloat16 [4096, 1024], P('fsdp'), may hold values from -6 to 6
- momentum: bfloat16 [4096, 1024], P('fsdp'), may hold values from -3 to 3
Outputs:
- new_params: bfloat16 [4096, 1024], replicated
- new_momentum: bfloat16 [4096, 1024], P('fsdp')
All inputs are finite; a program needn't handle non-finite values.
Results may differ from a plain program's by a relative error of at most 0.006.
Values may be sent and summed in bfloat16 or wider, within the bound.
A program may use at most 64 MiB of HBM per device.

v0:
```python
import jax
import jax.numpy as jnp
from jax import lax
from jax.sharding import Mesh
from jax.sharding import PartitionSpec as P

REP = ("rep_0", "rep_1", "rep_2")


def filled_up(lines, peers):
    spare = -len(lines) % peers
    return jnp.pad(lines, [(0, spare)] + [(0, 0)] * (lines.ndim - 1))


def sent_to_all(shard, axis):
    copies = jnp.broadcast_to(shard, (lax.axis_size(axis), *shard.shape))
    return lax.all_to_all(copies, axis, split_axis=0, concat_axis=0, tiled=True)


def joined_along(blocks, dim):
    blocks = jnp.moveaxis(blocks, 0, dim)
    lengths = blocks.shape
    return blocks.reshape(*lengths[:dim], lengths[dim] * lengths[dim + 1], *lengths[dim + 2 :])


def whole_of(shard, axes, dim):
    far, near = axes
    first = sent_to_all(shard, far)
    blocks = jnp.swapaxes(sent_to_all(first, near), 0, 1)
    return joined_along(blocks.reshape(-1, *shard.shape), dim)


def in_blocks(shard, dim, peers):
    before, after = (shard.shape[:dim], shard.shape[dim + 1 :])
    return jnp.moveaxis(shard.reshape(*before, peers, -1, *after), dim, 0)


def sum_at_owner(shard, axis, dim):
    blocks = in_blocks(shard, dim, lax.axis_size(axis))
    arrived = lax.all_to_all(blocks, axis, split_axis=0, concat_axis=0, tiled=True)
    return arrived.astype(jnp.float32).sum(axis=0)


def summed_rows(shard, axes, dim):
    far, near = axes
    own = sum_at_owner(in_blocks(shard, dim, lax.axis_size(far)), near, dim + 1)
    return jnp.sum(
        lax.all_to_all(own.astype(jnp.bfloat16), far, 0, 0, tiled=True).astype(jnp.float32), axis=0
    )


def sum_by_parts(shard, axes):
    lines = shard.reshape(-1, shard.shape[-1])
    padded = filled_up(lines, lax.axis_size(axes[0]) * lax.axis_size(axes[1]))
    whole = whole_of(summed_rows(padded, axes, 0).astype(jnp.bfloat16), axes, 0)
    return lax.slice_in_dim(whole, 0, len(lines)).reshape(shard.shape).astype(jnp.float32)


def dequantize(code_rows, scale_rows):
    count, width = code_rows.shape
    pieces = (
        code_rows.astype(jnp.float32).reshape(count, width // 128, 128) * scale_rows[:, :, None]
    )
    return pieces.reshape(count, width)


def outer_update(total, params, momentum, replicas):
    delta = total / replicas
    moment = 0.9 * momentum.astype(jnp.float32) + delta
    updated = (params.astype(jnp.float32) - 0.7 * (delta + 0.9 * moment)).astype(jnp.bfloat16)
    return (updated, moment.astype(jnp.bfloat16))


def local(codes, block_scales, params, momentum):
    replicas = lax.axis_size(REP)
    local_term = dequantize(codes[0], block_scales[0])
    total = sum_by_parts(local_term.astype(jnp.bfloat16), (("rep_0", "rep_1"), "rep_2"))
    updated, new_momentum = outer_update(total, params, momentum, replicas)
    new_params = lax.all_gather(updated, "fsdp", axis=0, tiled=True)
    return (new_params, new_momentum)


def solution(mesh):
    finer = Mesh(
        mesh.devices.reshape(4, 4, 2, mesh.shape["fsdp"]), ("rep_0", "rep_1", "rep_2", "fsdp")
    )
    placed = (P(REP, "fsdp", None), P(REP, "fsdp", None), P("fsdp", None), P("fsdp", None))
    return jax.shard_map(
        local, mesh=finer, in_specs=placed, out_specs=(P(), P("fsdp", None)), check_vma=False
    )
```

profile of v0, /device:TPU:1, one launch (start us, length us, event | category | flops | bytes accessed | tf_op | source)
XLA Modules:
  0.0 167.0 jit_solution(15279222004547587232)
XLA Ops:
  7.2 0.0 all-gather.2.cloned.1.call-start
  7.2 0.8 copy.11
  8.1 0.6 mul.27
  8.7 0.0 copy-start
  8.7 1.5 mul.28
  10.2 0.0 copy-done
  10.2 1.9 %fusion.5 = bf16[2,16,16,1024]{3,2,0,1:T(8,128)(2,1)S(1)} fusion(f32[16,2,16,1024]{3,2,1,0:T(8,128)} %mul.28, bf16[16,2,16,1024]{3,2,1,0:T(8,128)(2,1)S(1)} %bitcast.20), kind=kLoop, calls=%fused_computation.9 | loop fusion | flops 1572864 | bytes 4194304 | tf_op jit(solution)/shard_map/transpose | solution.py:35
  12.1 0.1 copy.12
  12.2 7.4 %all_to_all.20 = bf16[2,16,16,1024]{3,2,1,0:T(8,128)(2,1)S(1)} all-to-all(bf16[2,16,16,1024]{3,2,1,0:T(8,128)(2,1)S(1)} %copy.12), channel_id=1, replica_groups=mesh['rep_0'=4,'rep_1'=4,'rep_2'=2,'fsdp'=8] {'rep_2'}, dimensions={0} | all-to-all | bytes 2097152 | tf_op jit(solution)/shard_map/all_to_all | solution.py:40
  19.6 0.3 reduce_sum.24
  19.9 15.5 %all_to_all.21 = bf16[16,16,1024]{2,1,0:T(8,128)(2,1)S(1)} all-to-all(bf16[16,16,1024]{2,1,0:T(8,128)(2,1)S(1)} %reduce_sum.24), channel_id=1, replica_groups=mesh['rep_0'=4,'rep_1'=4,'rep_2'=2,'fsdp'=8] {'rep_0','rep_1'}, dimensions={0} | all-to-all | bytes 1048576 | tf_op jit(solution)/shard_map/all_to_all | solution.py:48
  35.4 0.1 reduce_sum.25
  35.5 0.1 broadcast_in_dim.6
  35.6 13.4 %all_to_all.22 = bf16[16,16,1024]{2,1,0:T(8,128)(2,1)S(1)} all-to-all(bf16[16,16,1024]{2,1,0:T(8,128)(2,1)S(1)} %broadcast_in_dim.6), channel_id=1, replica_groups=mesh['rep_0'=4,'rep_1'=4,'rep_2'=2,'fsdp'=8] {'rep_0','rep_1'}, dimensions={0} | all-to-all | bytes 1048576 | tf_op jit(solution)/shard_map/all_to_all | solution.py:17
  49.0 0.1 broadcast_in_dim.7
  49.1 6.5 %all_to_all.23 = bf16[2,16,16,1024]{3,2,1,0:T(8,128)(2,1)S(1)} all-to-all(bf16[2,16,16,1024]{3,2,1,0:T(8,128)(2,1)S(1)} %broadcast_in_dim.7), channel_id=1, replica_groups=mesh['rep_0'=4,'rep_1'=4,'rep_2'=2,'fsdp'=8] {'rep_2'}, dimensions={0} | all-to-all | bytes 2097152 | tf_op jit(solution)/shard_map/all_to_all | solution.py:17
  55.7 0.0 copy-start.1
  55.7 0.3 convert_multiply_fusion.1
  55.9 1.0 copy-done.1
  56.9 0.3 copy-done.2
  57.2 2.0 %fusion.4 = (bf16[512,1024]{1,0:T(8,128)(2,1)}, bf16[512,1024]{1,0:T(8,128)(2,1)}) fusion(f32[2,16,16,1024]{3,2,0,1:T(8,128)S(1)} %convert_multiply_fusion.1, bf16[512,1024]{1,0:T(8,128)(2,1)S(1)} %copy-done.1, bf16[512,1024]{1,0:T(8,128)(2,1)S(1)} %copy-done.2), kind=kLoop, calls=%fused_computation.7 | loop fusion | flops 5242880 | bytes 6291456 | tf_op jit(solution)/shard_map/convert_element_type | solution.py:71
  59.3 0.0 all-gather.2.cloned.1.call-update
  59.3 93.1 %all-gather.2.cloned.1.call-done = bf16[4096,1024]{1,0:T(8,128)(2,1)} async-done(((bf16[512,1024]{1,0:T(8,128)(2,1)}), bf16[4096,1024]{1,0:T(8,128)(2,1)}) %all-gather.2.cloned.1.call-update) | async-done | bytes 8388624 | tf_op jit(solution)/shard_map/all_gather | solution.py:79
  152.4 7.8 %copy.16 = bf16[4096,1024]{1,0:T(8,128)(2,1)} copy(bf16[4096,1024]{1,0:T(8,128)(2,1)} %all-gather.2.cloned.1.call-done) | data formatting | bytes 16777216
  (1 shorter events, 0.0 us)
Async XLA Ops:
  7.2 145.2 %all-gather.2.cloned.1.call-start = ((), (), s32[]{:S(2)}) async-start(), calls=%async_computation.4 | async-start | bytes 9437184 | tf_op jit(solution)/shard_map/all_gather | solution.py:79
  8.7 1.5 copy-start
  55.7 1.2 copy-start.1
  55.7 1.5 copy-start.2
Sparse Core Ops, SparseCore 0:
  59.4 92.9 all-gather.1
where the time goes:
time: 167 us
  waiting for transfers between devices  93.1 us (56%)
  blocking collectives  42.9 us (26%)
  between operations  14.1 us (8%)
  local copies, waits for them, and re-layouts  12.2 us (7%)
  other arithmetic  4.57 us (3%)
    all_gather x1, waiting for transfers between devices, local(): new_params = lax.all_gather(updated, 'fsdp', axis=0, tiled=True)  93.1 us
    all_to_all x2, blocking collectives, sent_to_all(): return lax.all_to_all(copies, axis, split_axis=0, concat_axis=0, tiled=True)  20 us
    all_to_all x1, blocking collectives, summed_rows(): lax.all_to_all(own.astype(jnp.bfloat16), far, 0, 0, tiled=True)  15.5 us
    unnamed x7, local copies, waits for them, and re-layouts  9.05 us
    all_to_all x1, blocking collectives, sum_at_owner(): lax.all_to_all(blocks, axis, split_axis=0, concat_axis=0, tiled=True)  7.44 us
  transfers between devices with their start and end apart: 1, of which 1 were waited for; matrix products, arithmetic and copies ran while one was open for 0% of the time, Pallas kernels for 0%

commit v1 on v0

--- a/solution.py
+++ b/solution.py
@@ -76,7 +76,23 @@
     local_term = dequantize(codes[0], block_scales[0])
     total = sum_by_parts(local_term.astype(jnp.bfloat16), (("rep_0", "rep_1"), "rep_2"))
     updated, new_momentum = outer_update(total, params, momentum, replicas)
-    new_params = lax.all_gather(updated, "fsdp", axis=0, tiled=True)
+    w1, b_next, carry_in = (lax.psum(1, "fsdp"), lax.axis_index("fsdp"), updated.shape[0])
+    lanes = tuple(((to_i, (to_i + 1) % w1) for to_i in range(w1)))
+    series = tuple(((to_i, (to_i - 1) % w1) for to_i in range(w1)))
+    new_params = jnp.zeros((*updated.shape[:0], w1 * carry_in, *updated.shape[1:]), updated.dtype)
+    new_params = lax.dynamic_update_slice_in_dim(new_params, updated, b_next * carry_in, axis=0)
+    e_now = front = updated
+    everything = w1 // 2
+    for b in [*range(1, everything + 1)]:
+        e_now = lax.ppermute(e_now, "fsdp", lanes)
+        new_params = lax.dynamic_update_slice_in_dim(
+            new_params, e_now, (b_next - b) % w1 * carry_in, axis=0
+        )
+        if b < w1 - everything:
+            front = lax.ppermute(front, "fsdp", series)
+            new_params = lax.dynamic_update_slice_in_dim(
+                new_params, front, (b_next + b) % w1 * carry_in, axis=0
+            )
     return (new_params, new_momentum)
 
 

time: 167 us -> 159 us (0.952)
  between operations: 14.1 us -> 0.83 us
  starting transfers between devices: 0.04 us -> 9.98 us
  waiting for transfers between devices: 93.1 us -> 84.9 us
  local copies, waits for them, and re-layouts: 12.2 us -> 14.4 us
    all_gather x1 -> x0, waiting for transfers between devices: 93.1 us -> none  [local(): new_params = lax.all_gather(updated, 'fsdp', axis=0, tiled=True)]
    ppermute x0 -> x7, waiting for transfers between devices: none -> 84.9 us  [the longest x4 84.9 us: local(): e_now = lax.ppermute(e_now, 'fsdp', lanes)]
    ppermute x0 -> x7, starting transfers between devices: none -> 9.98 us  [the longest x3 8.33 us: local(): front = lax.ppermute(front, 'fsdp', series)]
    dynamic_update_slice x0 -> x8, local copies, waits for them, and re-layouts: none -> 5.78 us  [the longest x4 2.89 us: local(): lax.dynamic_update_slice_in_dim(new_params, e_now, (b_next - b) % w1 * ca...]
    unnamed x7 -> x10, local copies, waits for them, and re-layouts: 9.05 us -> 4.37 us
  transfers between devices with their start and end apart: 1 -> 7, of which waited for: 1 -> 4; matrix products, arithmetic and copies ran while one was open for 0% -> 3% of each run, Pallas kernels for 0% -> 0%
where the time goes in v1:
time: 159 us; the launch traced here: 158 us
  waiting for transfers between devices  84.9 us (53%)
  blocking collectives  43.2 us (27%)
  local copies, waits for them, and re-layouts  14.4 us (9%)
  starting transfers between devices  9.98 us (6%)
  other arithmetic  4.5 us (3%)
    ppermute x4, waiting for transfers between devices, local(): e_now = lax.ppermute(e_now, 'fsdp', lanes)  84.9 us
    all_to_all x2, blocking collectives, sent_to_all(): return lax.all_to_all(copies, axis, split_axis=0, concat_axis=0, tiled=True)  20.1 us
    all_to_all x1, blocking collectives, summed_rows(): lax.all_to_all(own.astype(jnp.bfloat16), far, 0, 0, tiled=True)  15.5 us
    ppermute x3, starting transfers between devices, local(): front = lax.ppermute(front, 'fsdp', series)  8.33 us
    all_to_all x1, blocking collectives, sum_at_owner(): lax.all_to_all(blocks, axis, split_axis=0, concat_axis=0, tiled=True)  7.57 us
    unnamed x10, local copies, waits for them, and re-layouts  4.37 us
  transfers between devices with their start and end apart: 7, of which 4 were waited for; matrix products, arithmetic and copies ran while one was open for 3% of the time, Pallas kernels for 0%

profile of v1, /device:TPU:1, one launch (start us, length us, event | category | flops | bytes accessed | tf_op | source)
XLA Modules:
  0.0 157.8 jit_solution(3993037455809358906)
XLA Ops:
  0.6 0.8 copy.11
  1.5 0.6 mul.51
  2.1 1.5 mul.52
  3.6 2.2 %fusion.5 = bf16[2,16,16,1024]{3,2,0,1:T(8,128)(2,1)S(1)} fusion(f32[16,2,16,1024]{3,2,1,0:T(8,128)} %mul.52, bf16[16,2,16,1024]{3,2,1,0:T(8,128)(2,1)} %bitcast.20), kind=kLoop, calls=%fused_computation.9 | loop fusion | flops 1572864 | bytes 4194304 | tf_op jit(solution)/shard_map/transpose | solution.py:35
  5.9 7.6 %all_to_all.20 = bf16[2,16,16,1024]{3,2,1,0:T(8,128)(2,1)S(1)} all-to-all(bf16[2,16,16,1024]{3,2,1,0:T(8,128)(2,1)S(1)} %copy.12), channel_id=1, replica_groups=mesh['rep_0'=4,'rep_1'=4,'rep_2'=2,'fsdp'=8] {'rep_2'}, dimensions={0} | all-to-all | bytes 2097152 | tf_op jit(solution)/shard_map/all_to_all | solution.py:40
  13.7 15.5 %all_to_all.21 = bf16[16,16,1024]{2,1,0:T(8,128)(2,1)S(1)} all-to-all(bf16[16,16,1024]{2,1,0:T(8,128)(2,1)S(1)} %reduce_sum.24), channel_id=1, replica_groups=mesh['rep_0'=4,'rep_1'=4,'rep_2'=2,'fsdp'=8] {'rep_0','rep_1'}, dimensions={0} | all-to-all | bytes 1048576 | tf_op jit(solution)/shard_map/all_to_all | solution.py:48
  29.4 13.6 %all_to_all.22 = bf16[16,16,1024]{2,1,0:T(8,128)(2,1)S(1)} all-to-all(bf16[16,16,1024]{2,1,0:T(8,128)(2,1)S(1)} %broadcast_in_dim.10), channel_id=1, replica_groups=mesh['rep_0'=4,'rep_1'=4,'rep_2'=2,'fsdp'=8] {'rep_0','rep_1'}, dimensions={0} | all-to-all | bytes 1048576 | tf_op jit(solution)/shard_map/all_to_all | solution.py:17
  43.1 6.5 %all_to_all.23 = bf16[2,16,16,1024]{3,2,1,0:T(8,128)(2,1)S(1)} all-to-all(bf16[2,16,16,1024]{3,2,1,0:T(8,128)(2,1)S(1)} %broadcast_in_dim.11), channel_id=1, replica_groups=mesh['rep_0'=4,'rep_1'=4,'rep_2'=2,'fsdp'=8] {'rep_2'}, dimensions={0} | all-to-all | bytes 2097152 | tf_op jit(solution)/shard_map/all_to_all | solution.py:17
  49.9 1.7 %fusion.4 = (bf16[512,1024]{1,0:T(8,128)(2,1)}, bf16[512,1024]{1,0:T(8,128)(2,1)S(1)}) fusion(f32[2,16,16,1024]{3,2,0,1:T(8,128)S(1)} %convert_multiply_fusion.1, bf16[512,1024]{1,0:T(8,128)(2,1)S(1)} %copy-done.3, bf16[512,1024]{1,0:T(8,128)(2,1)S(1)} %copy-done.4), kind=kLoop, calls=%fused_computation.7 | loop fusion | flops 5242880 | bytes 6291456 | tf_op jit(solution)/shard_map/convert_element_type | solution.py:71
  51.6 1.6 %collective-permute-start = (bf16[512,1024]{1,0:T(8,128)(2,1)S(1)}, bf16[512,1024]{1,0:T(8,128)(2,1)S(1)}, u32[]{:S(2)}, u32[]{:S(2)}) collective-permute-start(bf16[512,1024]{1,0:T(8,128)(2,1)S(1)} %get-tuple-element.3), channel_id=1, source_target_pairs={{0,1},{1,2},{2,3},{3,4},{4,5},{5,6},{6,7},{7,0},{8,9},{9,10},{10,1... | collective-permute-start | bytes 3145736 | tf_op jit(solution)/shard_map/ppermute | solution.py:87
  53.2 3.9 %collective-permute-start.1 = (bf16[512,1024]{1,0:T(8,128)(2,1)S(1)}, bf16[512,1024]{1,0:T(8,128)(2,1)S(1)}, u32[]{:S(2)}, u32[]{:S(2)}) collective-permute-start(bf16[512,1024]{1,0:T(8,128)(2,1)S(1)} %get-tuple-element.3), channel_id=1, source_target_pairs={{0,7},{1,0},{2,1},{3,2},{4,3},{5,4},{6,5},{7,6},{8,15},{9,8},{10,9... | collective-permute-start | bytes 3145736 | tf_op jit(solution)/shard_map/ppermute | solution.py:92
  57.2 23.2 %collective-permute-done = bf16[512,1024]{1,0:T(8,128)(2,1)S(1)} collective-permute-done((bf16[512,1024]{1,0:T(8,128)(2,1)S(1)}, bf16[512,1024]{1,0:T(8,128)(2,1)S(1)}, u32[]{:S(2)}, u32[]{:S(2)}) %collective-permute-start) | collective-permute-done | bytes 1048608 | tf_op jit(solution)/shard_map/ppermute | solution.py:87
  80.4 2.7 %collective-permute-start.3 = (bf16[512,1024]{1,0:T(8,128)(2,1)S(1)}, bf16[512,1024]{1,0:T(8,128)(2,1)}, u32[]{:S(2)}, u32[]{:S(2)}) collective-permute-start(bf16[512,1024]{1,0:T(8,128)(2,1)S(1)} %collective-permute-done.1), channel_id=1, source_target_pairs={{0,7},{1,0},{2,1},{3,2},{4,3},{5,4},{6,5},{7,6},{8,15},{9,8},{10,9... | collective-permute-start | bytes 3145736 | tf_op jit(solution)/shard_map/ppermute | solution.py:92
  83.1 22.3 %collective-permute-done.2 = bf16[512,1024]{1,0:T(8,128)(2,1)S(1)} collective-permute-done((bf16[512,1024]{1,0:T(8,128)(2,1)S(1)}, bf16[512,1024]{1,0:T(8,128)(2,1)S(1)}, u32[]{:S(2)}, u32[]{:S(2)}) %collective-permute-start.2) | collective-permute-done | bytes 1048608 | tf_op jit(solution)/shard_map/ppermute | solution.py:87
  105.4 1.0 copy-done.1
  106.4 1.7 %collective-permute-start.5 = (bf16[512,1024]{1,0:T(8,128)(2,1)}, bf16[512,1024]{1,0:T(8,128)(2,1)}, u32[]{:S(2)}, u32[]{:S(2)}) collective-permute-start(bf16[512,1024]{1,0:T(8,128)(2,1)} %collective-permute-done.3), channel_id=1, source_target_pairs={{0,7},{1,0},{2,1},{3,2},{4,3},{5,4},{6,5},{7,6},{8,15},{9,8},{10,9... | collective-permute-start | bytes 3145736 | tf_op jit(solution)/shard_map/ppermute | solution.py:92
  108.1 21.5 %collective-permute-done.4 = bf16[512,1024]{1,0:T(8,128)(2,1)} collective-permute-done((bf16[512,1024]{1,0:T(8,128)(2,1)S(1)}, bf16[512,1024]{1,0:T(8,128)(2,1)}, u32[]{:S(2)}, u32[]{:S(2)}) %collective-permute-start.4) | collective-permute-done | bytes 1048608 | tf_op jit(solution)/shard_map/ppermute | solution.py:87
  129.6 1.1 broadcast_in_dim.9
  131.2 1.3 constant_dynamic-update-slice_fusion.3
  132.5 1.3 constant_dynamic-update-slice_fusion.2
  133.9 1.3 constant_dynamic-update-slice_fusion.1
  135.2 17.9 %collective-permute-done.6 = bf16[512,1024]{1,0:T(8,128)(2,1)} collective-permute-done((bf16[512,1024]{1,0:T(8,128)(2,1)}, bf16[512,1024]{1,0:T(8,128)(2,1)}, u32[]{:S(2)}, u32[]{:S(2)}) %collective-permute-start.6) | collective-permute-done | bytes 1048608 | tf_op jit(solution)/shard_map/ppermute | solution.py:87
  153.1 1.3 constant_dynamic-update-slice_fusion
  154.4 3.4 %copy-done = bf16[4096,1024]{1,0:T(8,128)(2,1)} copy-done((bf16[4096,1024]{1,0:T(8,128)(2,1)}, bf16[4096,1024]{1,0:T(8,128)(2,1)S(1)}, u32[]{:S(2)}) %copy-start) | copy-done | bytes 8388632
  (24 shorter events, 1.3 us)
Async XLA Ops:
  5.8 44.1 %copy-start.3 = (bf16[512,1024]{1,0:T(8,128)(2,1)S(1)}, bf16[512,1024]{1,0:T(8,128)(2,1)}, u32[]{:S(2)}) copy-start(bf16[512,1024]{1,0:T(8,128)(2,1)} %param.7) | copy-start | bytes 3145732
  29.3 20.6 %copy-start.4 = (bf16[512,1024]{1,0:T(8,128)(2,1)S(1)}, bf16[512,1024]{1,0:T(8,128)(2,1)}, u32[]{:S(2)}) copy-start(bf16[512,1024]{1,0:T(8,128)(2,1)} %param.6) | copy-start | bytes 3145732
  51.6 28.8 %collective-permute-start = (bf16[512,1024]{1,0:T(8,128)(2,1)S(1)}, bf16[512,1024]{1,0:T(8,128)(2,1)S(1)}, u32[]{:S(2)}, u32[]{:S(2)}) collective-permute-start(bf16[512,1024]{1,0:T(8,128)(2,1)S(1)} %get-tuple-element.3), channel_id=1, source_target_pairs={{0,1},{1,2},{2,3},{3,4},{4,5},{5,6},{6,7},{7,0},{8,9},{9,10},{10,1... | collective-permute-start | bytes 3145736 | tf_op jit(solution)/shard_map/ppermute | solution.py:87
  53.2 27.2 %collective-permute-start.1 = (bf16[512,1024]{1,0:T(8,128)(2,1)S(1)}, bf16[512,1024]{1,0:T(8,128)(2,1)S(1)}, u32[]{:S(2)}, u32[]{:S(2)}) collective-permute-start(bf16[512,1024]{1,0:T(8,128)(2,1)S(1)} %get-tuple-element.3), channel_id=1, source_target_pairs={{0,7},{1,0},{2,1},{3,2},{4,3},{5,4},{6,5},{7,6},{8,15},{9,8},{10,9... | collective-permute-start | bytes 3145736 | tf_op jit(solution)/shard_map/ppermute | solution.py:92
  80.4 25.0 %collective-permute-start.2 = (bf16[512,1024]{1,0:T(8,128)(2,1)S(1)}, bf16[512,1024]{1,0:T(8,128)(2,1)S(1)}, u32[]{:S(2)}, u32[]{:S(2)}) collective-permute-start(bf16[512,1024]{1,0:T(8,128)(2,1)S(1)} %collective-permute-done), channel_id=1, source_target_pairs={{0,1},{1,2},{2,3},{3,4},{4,5},{5,6},{6,7},{7,0},{8,9},{9,10},{10,1... | collective-permute-start | bytes 3145736 | tf_op jit(solution)/shard_map/ppermute | solution.py:87
  80.4 25.0 %collective-permute-start.3 = (bf16[512,1024]{1,0:T(8,128)(2,1)S(1)}, bf16[512,1024]{1,0:T(8,128)(2,1)}, u32[]{:S(2)}, u32[]{:S(2)}) collective-permute-start(bf16[512,1024]{1,0:T(8,128)(2,1)S(1)} %collective-permute-done.1), channel_id=1, source_target_pairs={{0,7},{1,0},{2,1},{3,2},{4,3},{5,4},{6,5},{7,6},{8,15},{9,8},{10,9... | collective-permute-start | bytes 3145736 | tf_op jit(solution)/shard_map/ppermute | solution.py:92
  105.4 1.0 copy-start.1
  105.4 24.2 %collective-permute-start.4 = (bf16[512,1024]{1,0:T(8,128)(2,1)S(1)}, bf16[512,1024]{1,0:T(8,128)(2,1)}, u32[]{:S(2)}, u32[]{:S(2)}) collective-permute-start(bf16[512,1024]{1,0:T(8,128)(2,1)S(1)} %collective-permute-done.2), channel_id=1, source_target_pairs={{0,1},{1,2},{2,3},{3,4},{4,5},{5,6},{6,7},{7,0},{8,9},{9,10},{10,1... | collective-permute-start | bytes 3145736 | tf_op jit(solution)/shard_map/ppermute | solution.py:87
  106.4 27.5 %collective-permute-start.5 = (bf16[512,1024]{1,0:T(8,128)(2,1)}, bf16[512,1024]{1,0:T(8,128)(2,1)}, u32[]{:S(2)}, u32[]{:S(2)}) collective-permute-start(bf16[512,1024]{1,0:T(8,128)(2,1)} %collective-permute-done.3), channel_id=1, source_target_pairs={{0,7},{1,0},{2,1},{3,2},{4,3},{5,4},{6,5},{7,6},{8,15},{9,8},{10,9... | collective-permute-start | bytes 3145736 | tf_op jit(solution)/shard_map/ppermute | solution.py:92
  129.6 23.5 %collective-permute-start.6 = (bf16[512,1024]{1,0:T(8,128)(2,1)}, bf16[512,1024]{1,0:T(8,128)(2,1)}, u32[]{:S(2)}, u32[]{:S(2)}) collective-permute-start(bf16[512,1024]{1,0:T(8,128)(2,1)} %collective-permute-done.4), channel_id=1, source_target_pairs={{0,1},{1,2},{2,3},{3,4},{4,5},{5,6},{6,7},{7,0},{8,9},{9,10},{10,1... | collective-permute-start | bytes 3145736 | tf_op jit(solution)/shard_map/ppermute | solution.py:87
  129.6 1.4 copy-start.2
  154.4 3.4 %copy-start = (bf16[4096,1024]{1,0:T(8,128)(2,1)}, bf16[4096,1024]{1,0:T(8,128)(2,1)S(1)}, u32[]{:S(2)}) copy-start(bf16[4096,1024]{1,0:T(8,128)(2,1)S(1)} %constant_dynamic-update-slice_fusion) | copy-start | bytes 25165828
